TPU v7x, 32 devices: a whole 2x2x4 slice. The times are simulated.
32 devices in a mesh: blk: 8 (over z, x), rep: 4 (over y, core).
Axes of the slice: x: 2, y: 2, z: 4, core: 2. Of those that a mesh axis runs over, the one named last changes fastest.
Arguments:
- features: bfloat16 [8192, 256], P(('blk', 'rep')), may hold values from -6 to 6
- weight: bfloat16 [256, 256], replicated, may hold values from -0.375 to 0.375
- pre_cot: bfloat16 [8192, 256], P(('blk', 'rep')), may hold values from -6 to 6
- tile_count: int32 [8, 4, 8], P('blk', 'rep'), may hold values from 0 to 2, as said below
- tile_rowid: int32 [8, 4, 8, 2], P('blk', 'rep'), may hold values from 0 to 3, as said below
- edge_cols: int32 [8, 4, 8, 2, 1, 256], P('blk', 'rep'), may hold values from 0 to 255
- edge_vals: bfloat16 [8, 4, 8, 2, 1, 256], P('blk', 'rep'), may hold values from -1.25 to 1.25
Outputs:
- activations: bfloat16 [8192, 256], P(('blk', 'rep'))
- grad_weight: float32 [256, 256], replicated
Inputs may be any that keep to these rules, and one draw needn't show every extreme that they name: `tile_count`: the panel p = b always has all 2 slots live. `tile_rowid`: the 2 slots of one block row, tile position and panel name distinct row tiles.
All inputs are finite; a program needn't handle non-finite values.
Results may differ from a plain program's by a relative error of at most 0.011.
Values may be sent and summed in bfloat16 or wider, within the bound.
A program may use at most 64 MiB of HBM per device.

v0:
```python
import jax
import jax.numpy as jnp
from jax import lax
from jax.sharding import PartitionSpec as P


def shifted(array, axis, by):
    count = lax.axis_size(axis)
    return lax.ppermute(array, axis, [(i, (i + by) % count) for i in range(count)])


def shards(features, weight, pre_cot, tile_count, tile_rowid, edge_cols, edge_vals):
    tile_rows = features.shape[0]
    feat_width = features.shape[1]
    rep_count = lax.axis_size("rep")
    blocks = lax.axis_size("blk")
    home_index = lax.axis_index("blk")
    counts = tile_count.reshape(-1)
    row_ids = tile_rowid.reshape(tile_rowid.shape[2], tile_rowid.shape[3])
    edge_index = edge_cols.reshape(edge_cols.shape[2:])
    edge_weight = edge_vals.reshape(edge_vals.shape[2:])
    slot_count = edge_index.shape[1]
    columns = lax.broadcasted_iota(jnp.int32, (1, 1, 1, tile_rows), 3)
    slot_ids = jnp.arange(slot_count, dtype=jnp.int32)
    zero_weight = jnp.zeros((), jnp.bfloat16)
    totals_start = jnp.zeros((rep_count * tile_rows, feat_width), jnp.float32)

    def apply_panel(totals, panel_now, panel_index):
        index_now = lax.dynamic_index_in_dim(edge_index, panel_index, 0, keepdims=False)
        weight_now = lax.dynamic_index_in_dim(edge_weight, panel_index, 0, keepdims=False)
        dense_tiles = jnp.sum(
            jnp.where(index_now[..., None] == columns, weight_now[..., None], zero_weight), axis=1
        )
        products = jnp.einsum(
            "sij,jf->sif", dense_tiles, panel_now, preferred_element_type=jnp.float32
        )
        live_mask = (slot_ids < counts[panel_index]).astype(jnp.float32)
        slot_rows = lax.dynamic_index_in_dim(row_ids, panel_index, 0, keepdims=False)
        for slot in range(slot_count):
            row_start = slot_rows[slot] * tile_rows
            current = lax.dynamic_slice_in_dim(totals, row_start, tile_rows, 0)
            totals = lax.dynamic_update_slice_in_dim(
                totals, current + products[slot] * live_mask[slot], row_start, 0
            )
        return totals

    totals = apply_panel(totals_start, features, home_index)

    def cycle_turn(turn_index, carry):
        totals_now, panel_now = carry
        panel_now = shifted(panel_now, "blk", 1)
        totals_now = apply_panel(totals_now, panel_now, (home_index - turn_index) % blocks)
        return (totals_now, panel_now)

    totals, _ = lax.fori_loop(1, blocks, cycle_turn, (totals, features))
    summed = lax.psum_scatter(totals.astype(jnp.bfloat16), "rep", scatter_dimension=0, tiled=True)
    preact = jnp.dot(summed, weight, preferred_element_type=jnp.float32)
    activations = jnp.maximum(preact, 0.0).astype(jnp.bfloat16)
    local_grad = lax.dot_general(
        summed, pre_cot, (((0,), (0,)), ((), ())), preferred_element_type=jnp.float32
    )
    total_grad = lax.psum(local_grad, ("blk", "rep"))
    node_total = blocks * rep_count * tile_rows
    grad_weight = total_grad * node_total ** (-0.5)
    return (activations, grad_weight)


def solution(mesh):
    in_specs = (
        P(("blk", "rep"), None),
        P(),
        P(("blk", "rep"), None),
        P("blk", "rep", None),
        P("blk", "rep", None, None),
        P("blk", "rep", None, None, None, None),
        P("blk", "rep", None, None, None, None),
    )
    out_specs = (P(("blk", "rep"), None), P())
    return jax.shard_map(shards, mesh=mesh, in_specs=in_specs, out_specs=out_specs, check_vma=False)
```

profile of v0, /device:TPU:0, one launch (start us, length us, event | category | flops | bytes accessed | tf_op | source)
XLA Modules:
  0.0 244.4 jit_solution(1695783370558010207)
XLA Ops:
  7.2 0.9 copy.30
  15.6 67.5 %while.18 = (s32[]{:T(128)}, f32[1024,256]{1,0:T(8,128)S(1)}, bf16[256,256]{1,0:T(8,128)(2,1)S(1)}, s32[]{:T(128)}, s32[8,2]{0,1:T(2,128)S(1)}, /*index=5*/s32[8...) while((s32[]{:T(128)}, f32[1024,256]{1,0:T(8,128)S(1)}, ...), condition=%wide.region_1.2_spmd.clone, body=%wide.region_0.1_spmd.clone.sunk | while | flops 67633168 | bytes 3024392 | solution.py:55
  15.7 3.0 %collective-permute-start = (bf16[256,256]{1,0:T(8,128)(2,1)S(1)}, bf16[256,256]{1,0:T(8,128)(2,1)S(1)}, u32[]{:S(2)}, u32[]{:S(2)}) collective-permute-start(bf16[256,256]{1,0:T(8,128)(2,1)S(1)} %get-tuple-element.362), channel_id=1, source_target_pairs={{0,4},{4,8},{8,12},{12,16},{16,20},{20,24},{24,28},{28,0},{1,5},{5... | collective-permute-start | bytes 393224 | tf_op jit(solution)/shard_map/while/body/eval_jaxpr/ppermute | solution.py:9
  23.0 2.2 collective-permute-done
  26.1 0.7 fusion.58
  31.3 3.3 %collective-permute-done = bf16[256,256]{1,0:T(8,128)(2,1)S(1)} collective-permute-done((bf16[256,256]{1,0:T(8,128)(2,1)S(1)}, bf16[256,256]{1,0:T(8,128)(2,1)S(1)}, u32[]{:S(2)}, u32[]{:S(2)}) %collective-permute-start) | collective-permute-done | bytes 131104 | tf_op jit(solution)/shard_map/while/body/eval_jaxpr/ppermute | solution.py:9
  35.5 0.7 fusion.58
  40.7 3.3 %collective-permute-done = bf16[256,256]{1,0:T(8,128)(2,1)S(1)} collective-permute-done((bf16[256,256]{1,0:T(8,128)(2,1)S(1)}, bf16[256,256]{1,0:T(8,128)(2,1)S(1)}, u32[]{:S(2)}, u32[]{:S(2)}) %collective-permute-start) | collective-permute-done | bytes 131104 | tf_op jit(solution)/shard_map/while/body/eval_jaxpr/ppermute | solution.py:9
  44.9 0.7 fusion.58
  50.1 3.3 %collective-permute-done = bf16[256,256]{1,0:T(8,128)(2,1)S(1)} collective-permute-done((bf16[256,256]{1,0:T(8,128)(2,1)S(1)}, bf16[256,256]{1,0:T(8,128)(2,1)S(1)}, u32[]{:S(2)}, u32[]{:S(2)}) %collective-permute-start) | collective-permute-done | bytes 131104 | tf_op jit(solution)/shard_map/while/body/eval_jaxpr/ppermute | solution.py:9
  54.3 0.7 fusion.58
  59.5 3.3 %collective-permute-done = bf16[256,256]{1,0:T(8,128)(2,1)S(1)} collective-permute-done((bf16[256,256]{1,0:T(8,128)(2,1)S(1)}, bf16[256,256]{1,0:T(8,128)(2,1)S(1)}, u32[]{:S(2)}, u32[]{:S(2)}) %collective-permute-start) | collective-permute-done | bytes 131104 | tf_op jit(solution)/shard_map/while/body/eval_jaxpr/ppermute | solution.py:9
  63.7 0.7 fusion.58
  68.8 3.3 %collective-permute-done = bf16[256,256]{1,0:T(8,128)(2,1)S(1)} collective-permute-done((bf16[256,256]{1,0:T(8,128)(2,1)S(1)}, bf16[256,256]{1,0:T(8,128)(2,1)S(1)}, u32[]{:S(2)}, u32[]{:S(2)}) %collective-permute-start) | collective-permute-done | bytes 131104 | tf_op jit(solution)/shard_map/while/body/eval_jaxpr/ppermute | solution.py:9
  73.0 0.7 fusion.58
  78.2 3.3 %collective-permute-done = bf16[256,256]{1,0:T(8,128)(2,1)S(1)} collective-permute-done((bf16[256,256]{1,0:T(8,128)(2,1)S(1)}, bf16[256,256]{1,0:T(8,128)(2,1)S(1)}, u32[]{:S(2)}, u32[]{:S(2)}) %collective-permute-start) | collective-permute-done | bytes 131104 | tf_op jit(solution)/shard_map/while/body/eval_jaxpr/ppermute | solution.py:9
  82.4 0.7 fusion.58
  83.1 0.9 convert_element_type.34
  84.1 19.9 %reduce-scatter.2.cloned.1.call-done = bf16[256,256]{1,0:T(8,128)(2,1)} async-done(((bf16[1024,256]{1,0:T(8,128)(2,1)}), bf16[256,256]{1,0:T(8,128)(2,1)}) %reduce-scatter.2.cloned.1.call-update) | async-done | bytes 131088 | tf_op jit(solution)/shard_map/reduce_scatter | solution.py:56
  104.0 1.8 fusion.38
  105.8 0.9 copy-done.1
  106.8 0.8 fusion.19
  107.6 128.3 %all-reduce.2.cloned.1.call-done = f32[256,256]{1,0:T(8,128)} async-done(((f32[256,256]{1,0:T(8,128)}), f32[256,256]{1,0:T(8,128)}) %all-reduce.2.cloned.1.call-update) | async-done | bytes 262160 | tf_op jit(solution)/shard_map/psum | solution.py:62
  235.9 1.7 broadcast_multiply_fusion
  (104 shorter events, 35.4 us)
Async XLA Ops:
  7.2 96.8 %copy-start = (bf16[256,256]{1,0:T(8,128)(2,1)S(1)}, bf16[256,256]{1,0:T(8,128)(2,1)}, u32[]{:S(2)}) copy-start(bf16[256,256]{1,0:T(8,128)(2,1)} %param.11) | copy-start | bytes 393220
  7.2 96.8 %reduce-scatter.2.cloned.1.call-start = ((), (), s32[]{:S(2)}) async-start(), calls=%async_computation.1 | async-start | bytes 655360 | tf_op jit(solution)/shard_map/reduce_scatter | solution.py:56
  8.2 0.7 copy-start.3
  8.2 2.5 %copy-start.4 = (s32[1,1,8,2,1,256]{5,4,3,2,1,0:T(1,128)S(1)}, s32[1,1,8,2,1,256]{5,4,3,2,1,0:T(1,128)}, u32[]{:S(2)}) copy-start(s32[1,1,8,2,1,256]{5,4,3,2,1,0:T(1,128)} %param.14) | copy-start | bytes 49156
  10.7 0.7 copy-start.5
  15.7 9.5 %collective-permute-start = (bf16[256,256]{1,0:T(8,128)(2,1)S(1)}, bf16[256,256]{1,0:T(8,128)(2,1)S(1)}, u32[]{:S(2)}, u32[]{:S(2)}) collective-permute-start(bf16[256,256]{1,0:T(8,128)(2,1)S(1)} %get-tuple-element.362), channel_id=1, source_target_pairs={{0,4},{4,8},{8,12},{12,16},{16,20},{20,24},{24,28},{28,0},{1,5},{5... | collective-permute-start | bytes 393224 | tf_op jit(solution)/shard_map/while/body/eval_jaxpr/ppermute | solution.py:9
  26.8 7.7 %collective-permute-start = (bf16[256,256]{1,0:T(8,128)(2,1)S(1)}, bf16[256,256]{1,0:T(8,128)(2,1)S(1)}, u32[]{:S(2)}, u32[]{:S(2)}) collective-permute-start(bf16[256,256]{1,0:T(8,128)(2,1)S(1)} %get-tuple-element.362), channel_id=1, source_target_pairs={{0,4},{4,8},{8,12},{12,16},{16,20},{20,24},{24,28},{28,0},{1,5},{5... | collective-permute-start | bytes 393224 | tf_op jit(solution)/shard_map/while/body/eval_jaxpr/ppermute | solution.py:9
  36.2 7.7 %collective-permute-start = (bf16[256,256]{1,0:T(8,128)(2,1)S(1)}, bf16[256,256]{1,0:T(8,128)(2,1)S(1)}, u32[]{:S(2)}, u32[]{:S(2)}) collective-permute-start(bf16[256,256]{1,0:T(8,128)(2,1)S(1)} %get-tuple-element.362), channel_id=1, source_target_pairs={{0,4},{4,8},{8,12},{12,16},{16,20},{20,24},{24,28},{28,0},{1,5},{5... | collective-permute-start | bytes 393224 | tf_op jit(solution)/shard_map/while/body/eval_jaxpr/ppermute | solution.py:9
  45.6 7.7 %collective-permute-start = (bf16[256,256]{1,0:T(8,128)(2,1)S(1)}, bf16[256,256]{1,0:T(8,128)(2,1)S(1)}, u32[]{:S(2)}, u32[]{:S(2)}) collective-permute-start(bf16[256,256]{1,0:T(8,128)(2,1)S(1)} %get-tuple-element.362), channel_id=1, source_target_pairs={{0,4},{4,8},{8,12},{12,16},{16,20},{20,24},{24,28},{28,0},{1,5},{5... | collective-permute-start | bytes 393224 | tf_op jit(solution)/shard_map/while/body/eval_jaxpr/ppermute | solution.py:9
  55.0 7.7 %collective-permute-start = (bf16[256,256]{1,0:T(8,128)(2,1)S(1)}, bf16[256,256]{1,0:T(8,128)(2,1)S(1)}, u32[]{:S(2)}, u32[]{:S(2)}) collective-permute-start(bf16[256,256]{1,0:T(8,128)(2,1)S(1)} %get-tuple-element.362), channel_id=1, source_target_pairs={{0,4},{4,8},{8,12},{12,16},{16,20},{20,24},{24,28},{28,0},{1,5},{5... | collective-permute-start | bytes 393224 | tf_op jit(solution)/shard_map/while/body/eval_jaxpr/ppermute | solution.py:9
  64.4 7.7 %collective-permute-start = (bf16[256,256]{1,0:T(8,128)(2,1)S(1)}, bf16[256,256]{1,0:T(8,128)(2,1)S(1)}, u32[]{:S(2)}, u32[]{:S(2)}) collective-permute-start(bf16[256,256]{1,0:T(8,128)(2,1)S(1)} %get-tuple-element.362), channel_id=1, source_target_pairs={{0,4},{4,8},{8,12},{12,16},{16,20},{20,24},{24,28},{28,0},{1,5},{5... | collective-permute-start | bytes 393224 | tf_op jit(solution)/shard_map/while/body/eval_jaxpr/ppermute | solution.py:9
  73.8 7.7 %collective-permute-start = (bf16[256,256]{1,0:T(8,128)(2,1)S(1)}, bf16[256,256]{1,0:T(8,128)(2,1)S(1)}, u32[]{:S(2)}, u32[]{:S(2)}) collective-permute-start(bf16[256,256]{1,0:T(8,128)(2,1)S(1)} %get-tuple-element.362), channel_id=1, source_target_pairs={{0,4},{4,8},{8,12},{12,16},{16,20},{20,24},{24,28},{28,0},{1,5},{5... | collective-permute-start | bytes 393224 | tf_op jit(solution)/shard_map/while/body/eval_jaxpr/ppermute | solution.py:9
  84.0 151.9 %all-reduce.2.cloned.1.call-start = ((), (), s32[]{:S(2)}) async-start(), calls=%async_computation.2 | async-start | bytes 524288 | tf_op jit(solution)/shard_map/psum | solution.py:62
  105.8 0.9 copy-start.1
  105.8 1.0 copy-start.2
Sparse Core Ops, SparseCore 0:
  84.1 19.7 reduce-scatter.1
  110.9 124.9 all-reduce.1
where the time goes:
time: 245 us; the launch traced here: 244 us
  waiting for transfers between devices  170 us (69%)
  local copies, waits for them, and re-layouts  23.5 us (10%)
  other arithmetic  18 us (7%)
  between operations  15.3 us (6%)
  loops' own time  8.9 us (4%)
  matrix products  5.24 us (2%)
  starting transfers between devices  3.42 us (1%)
    psum x1, waiting for transfers between devices, shards(): total_grad = lax.psum(local_grad, ('blk', 'rep'))  128 us
    ppermute x7, waiting for transfers between devices, shifted(): lax.ppermute(array, axis, [(i, (i + by) % count) for i in range(count)])  21.7 us
    reduce_scatter x1, waiting for transfers between devices, shards(): lax.psum_scatter(totals.astype(jnp.bfloat16), 'rep', scatter_dimension=0,...  19.9 us
    dynamic_update_slice x16, other arithmetic, apply_panel(): lax.dynamic_update_slice_in_dim(totals, current + products[slot] * live_m...  10.5 us
    another operation x1, loops' own time, shards(): totals, _ = lax.fori_loop(1, blocks, cycle_turn, (totals, features))  8.9 us
    broadcast_in_dim x8, local copies, waits for them, and re-layouts, apply_panel(): jnp.where(index_now[..., None] == columns, weight_now[..., None], zero_we...  5.45 us
    convert_element_type x8, other arithmetic, apply_panel(): live_mask = (slot_ids < counts[panel_index]).astype(jnp.float32)  5.04 us
    dynamic_slice x8, local copies, waits for them, and re-layouts, apply_panel(): live_mask = (slot_ids < counts[panel_index]).astype(jnp.float32)  4.95 us
  transfers between devices with their start and end apart: 9, of which 9 were waited for; matrix products, arithmetic and copies ran while one was open for 9% of the time, Pallas kernels for 0%

commit v1 on v0

--- a/solution.py
+++ b/solution.py
@@ -59,7 +59,7 @@
     local_grad = lax.dot_general(
         summed, pre_cot, (((0,), (0,)), ((), ())), preferred_element_type=jnp.float32
     )
-    total_grad = lax.psum(local_grad, ("blk", "rep"))
+    total_grad = lax.psum(lax.psum(local_grad, "rep"), "blk")
     node_total = blocks * rep_count * tile_rows
     grad_weight = total_grad * node_total ** (-0.5)
     return (activations, grad_weight)

time: 245 us -> 222 us (0.906)
  waiting for transfers between devices: 170 us -> 147 us
    psum x1 -> x2, waiting for transfers between devices: 128 us -> 105 us  [shards(): total_grad = lax.psum(lax.psum(local_grad, 'rep'), 'blk')]
  transfers between devices with their start and end apart: 9 -> 10, of which waited for: 9 -> 10; matrix products, arithmetic and copies ran while one was open for 9% -> 10% of each run, Pallas kernels for 0% -> 0%
where the time goes in v1:
time: 222 us; the launch traced here: 221 us
  waiting for transfers between devices  147 us (66%)
  local copies, waits for them, and re-layouts  23.5 us (11%)
  other arithmetic  18 us (8%)
  between operations  15 us (7%)
  loops' own time  8.9 us (4%)
  matrix products  5.24 us (2%)
  starting transfers between devices  3.46 us (2%)
    psum x2, waiting for transfers between devices, shards(): total_grad = lax.psum(lax.psum(local_grad, 'rep'), 'blk')  105 us
    ppermute x7, waiting for transfers between devices, shifted(): lax.ppermute(array, axis, [(i, (i + by) % count) for i in range(count)])  21.7 us
    reduce_scatter x1, waiting for transfers between devices, shards(): lax.psum_scatter(totals.astype(jnp.bfloat16), 'rep', scatter_dimension=0,...  19.9 us
    dynamic_update_slice x16, other arithmetic, apply_panel(): lax.dynamic_update_slice_in_dim(totals, current + products[slot] * live_m...  10.5 us
    another operation x1, loops' own time, shards(): totals, _ = lax.fori_loop(1, blocks, cycle_turn, (totals, features))  8.9 us
    broadcast_in_dim x8, local copies, waits for them, and re-layouts, apply_panel(): jnp.where(index_now[..., None] == columns, weight_now[..., None], zero_we...  5.45 us
    convert_element_type x8, other arithmetic, apply_panel(): live_mask = (slot_ids < counts[panel_index]).astype(jnp.float32)  5.04 us
    dynamic_slice x8, local copies, waits for them, and re-layouts, apply_panel(): live_mask = (slot_ids < counts[panel_index]).astype(jnp.float32)  4.95 us
  transfers between devices with their start and end apart: 10, of which 10 were waited for; matrix products, arithmetic and copies ran while one was open for 10% of the time, Pallas kernels for 0%

profile of v1, /device:TPU:0, one launch (start us, length us, event | category | flops | bytes accessed | tf_op | source)
XLA Modules:
  0.0 221.2 jit_solution(8673774227915816582)
XLA Ops:
  7.2 0.9 copy.31
  15.6 67.5 %while.18 = (s32[]{:T(128)}, f32[1024,256]{1,0:T(8,128)S(1)}, bf16[256,256]{1,0:T(8,128)(2,1)S(1)}, s32[]{:T(128)}, s32[8,2]{0,1:T(2,128)S(1)}, /*index=5*/s32[8...) while((s32[]{:T(128)}, f32[1024,256]{1,0:T(8,128)S(1)}, ...), condition=%wide.region_1.2_spmd.clone, body=%wide.region_0.1_spmd.clone.sunk | while | flops 67633168 | bytes 3024392 | solution.py:55
  15.7 3.0 %collective-permute-start = (bf16[256,256]{1,0:T(8,128)(2,1)S(1)}, bf16[256,256]{1,0:T(8,128)(2,1)S(1)}, u32[]{:S(2)}, u32[]{:S(2)}) collective-permute-start(bf16[256,256]{1,0:T(8,128)(2,1)S(1)} %get-tuple-element.362), channel_id=1, source_target_pairs={{0,4},{4,8},{8,12},{12,16},{16,20},{20,24},{24,28},{28,0},{1,5},{5... | collective-permute-start | bytes 393224 | tf_op jit(solution)/shard_map/while/body/eval_jaxpr/ppermute | solution.py:9
  23.0 2.2 collective-permute-done
  26.1 0.7 fusion.58
  31.3 3.3 %collective-permute-done = bf16[256,256]{1,0:T(8,128)(2,1)S(1)} collective-permute-done((bf16[256,256]{1,0:T(8,128)(2,1)S(1)}, bf16[256,256]{1,0:T(8,128)(2,1)S(1)}, u32[]{:S(2)}, u32[]{:S(2)}) %collective-permute-start) | collective-permute-done | bytes 131104 | tf_op jit(solution)/shard_map/while/body/eval_jaxpr/ppermute | solution.py:9
  35.5 0.7 fusion.58
  40.7 3.3 %collective-permute-done = bf16[256,256]{1,0:T(8,128)(2,1)S(1)} collective-permute-done((bf16[256,256]{1,0:T(8,128)(2,1)S(1)}, bf16[256,256]{1,0:T(8,128)(2,1)S(1)}, u32[]{:S(2)}, u32[]{:S(2)}) %collective-permute-start) | collective-permute-done | bytes 131104 | tf_op jit(solution)/shard_map/while/body/eval_jaxpr/ppermute | solution.py:9
  44.9 0.7 fusion.58
  50.1 3.3 %collective-permute-done = bf16[256,256]{1,0:T(8,128)(2,1)S(1)} collective-permute-done((bf16[256,256]{1,0:T(8,128)(2,1)S(1)}, bf16[256,256]{1,0:T(8,128)(2,1)S(1)}, u32[]{:S(2)}, u32[]{:S(2)}) %collective-permute-start) | collective-permute-done | bytes 131104 | tf_op jit(solution)/shard_map/while/body/eval_jaxpr/ppermute | solution.py:9
  54.3 0.7 fusion.58
  59.5 3.3 %collective-permute-done = bf16[256,256]{1,0:T(8,128)(2,1)S(1)} collective-permute-done((bf16[256,256]{1,0:T(8,128)(2,1)S(1)}, bf16[256,256]{1,0:T(8,128)(2,1)S(1)}, u32[]{:S(2)}, u32[]{:S(2)}) %collective-permute-start) | collective-permute-done | bytes 131104 | tf_op jit(solution)/shard_map/while/body/eval_jaxpr/ppermute | solution.py:9
  63.7 0.7 fusion.58
  68.8 3.3 %collective-permute-done = bf16[256,256]{1,0:T(8,128)(2,1)S(1)} collective-permute-done((bf16[256,256]{1,0:T(8,128)(2,1)S(1)}, bf16[256,256]{1,0:T(8,128)(2,1)S(1)}, u32[]{:S(2)}, u32[]{:S(2)}) %collective-permute-start) | collective-permute-done | bytes 131104 | tf_op jit(solution)/shard_map/while/body/eval_jaxpr/ppermute | solution.py:9
  73.0 0.7 fusion.58
  78.2 3.3 %collective-permute-done = bf16[256,256]{1,0:T(8,128)(2,1)S(1)} collective-permute-done((bf16[256,256]{1,0:T(8,128)(2,1)S(1)}, bf16[256,256]{1,0:T(8,128)(2,1)S(1)}, u32[]{:S(2)}, u32[]{:S(2)}) %collective-permute-start) | collective-permute-done | bytes 131104 | tf_op jit(solution)/shard_map/while/body/eval_jaxpr/ppermute | solution.py:9
  83.1 0.9 convert_element_type.34
  84.1 19.9 %reduce-scatter.2.cloned.1.call-done = bf16[256,256]{1,0:T(8,128)(2,1)} async-done(((bf16[1024,256]{1,0:T(8,128)(2,1)}), bf16[256,256]{1,0:T(8,128)(2,1)}) %reduce-scatter.2.cloned.1.call-update) | async-done | bytes 131088 | tf_op jit(solution)/shard_map/reduce_scatter | solution.py:56
  104.0 1.8 fusion.38
  105.9 33.1 %all-reduce.3.cloned.1.call-done = f32[256,256]{1,0:T(8,128)} async-done(((f32[256,256]{1,0:T(8,128)}), f32[256,256]{1,0:T(8,128)}) %all-reduce.3.cloned.1.call-update) | async-done | bytes 262160 | tf_op jit(solution)/shard_map/psum | solution.py:62
  139.0 0.9 copy-done.1
  139.9 0.8 fusion.19
  140.8 72.2 %all-reduce.5.cloned.1.call-done = f32[256,256]{1,0:T(8,128)} async-done(((f32[256,256]{1,0:T(8,128)}), f32[256,256]{1,0:T(8,128)}) %all-reduce.5.cloned.1.call-update) | async-done | bytes 262160 | tf_op jit(solution)/shard_map/psum | solution.py:62
  213.0 1.7 broadcast_multiply_fusion
  (107 shorter events, 36.2 us)
Async XLA Ops:
  7.2 96.8 %copy-start = (bf16[256,256]{1,0:T(8,128)(2,1)S(1)}, bf16[256,256]{1,0:T(8,128)(2,1)}, u32[]{:S(2)}) copy-start(bf16[256,256]{1,0:T(8,128)(2,1)} %param.11) | copy-start | bytes 393220
  7.2 96.8 %reduce-scatter.2.cloned.1.call-start = ((), (), s32[]{:S(2)}) async-start(), calls=%async_computation.1 | async-start | bytes 655360 | tf_op jit(solution)/shard_map/reduce_scatter | solution.py:56
  8.2 0.7 copy-start.3
  8.2 2.5 %copy-start.4 = (s32[1,1,8,2,1,256]{5,4,3,2,1,0:T(1,128)S(1)}, s32[1,1,8,2,1,256]{5,4,3,2,1,0:T(1,128)}, u32[]{:S(2)}) copy-start(s32[1,1,8,2,1,256]{5,4,3,2,1,0:T(1,128)} %param.14) | copy-start | bytes 49156
  10.7 0.7 copy-start.5
  15.7 9.5 %collective-permute-start = (bf16[256,256]{1,0:T(8,128)(2,1)S(1)}, bf16[256,256]{1,0:T(8,128)(2,1)S(1)}, u32[]{:S(2)}, u32[]{:S(2)}) collective-permute-start(bf16[256,256]{1,0:T(8,128)(2,1)S(1)} %get-tuple-element.362), channel_id=1, source_target_pairs={{0,4},{4,8},{8,12},{12,16},{16,20},{20,24},{24,28},{28,0},{1,5},{5... | collective-permute-start | bytes 393224 | tf_op jit(solution)/shard_map/while/body/eval_jaxpr/ppermute | solution.py:9
  26.8 7.7 %collective-permute-start = (bf16[256,256]{1,0:T(8,128)(2,1)S(1)}, bf16[256,256]{1,0:T(8,128)(2,1)S(1)}, u32[]{:S(2)}, u32[]{:S(2)}) collective-permute-start(bf16[256,256]{1,0:T(8,128)(2,1)S(1)} %get-tuple-element.362), channel_id=1, source_target_pairs={{0,4},{4,8},{8,12},{12,16},{16,20},{20,24},{24,28},{28,0},{1,5},{5... | collective-permute-start | bytes 393224 | tf_op jit(solution)/shard_map/while/body/eval_jaxpr/ppermute | solution.py:9
  36.2 7.7 %collective-permute-start = (bf16[256,256]{1,0:T(8,128)(2,1)S(1)}, bf16[256,256]{1,0:T(8,128)(2,1)S(1)}, u32[]{:S(2)}, u32[]{:S(2)}) collective-permute-start(bf16[256,256]{1,0:T(8,128)(2,1)S(1)} %get-tuple-element.362), channel_id=1, source_target_pairs={{0,4},{4,8},{8,12},{12,16},{16,20},{20,24},{24,28},{28,0},{1,5},{5... | collective-permute-start | bytes 393224 | tf_op jit(solution)/shard_map/while/body/eval_jaxpr/ppermute | solution.py:9
  45.6 7.7 %collective-permute-start = (bf16[256,256]{1,0:T(8,128)(2,1)S(1)}, bf16[256,256]{1,0:T(8,128)(2,1)S(1)}, u32[]{:S(2)}, u32[]{:S(2)}) collective-permute-start(bf16[256,256]{1,0:T(8,128)(2,1)S(1)} %get-tuple-element.362), channel_id=1, source_target_pairs={{0,4},{4,8},{8,12},{12,16},{16,20},{20,24},{24,28},{28,0},{1,5},{5... | collective-permute-start | bytes 393224 | tf_op jit(solution)/shard_map/while/body/eval_jaxpr/ppermute | solution.py:9
  55.0 7.7 %collective-permute-start = (bf16[256,256]{1,0:T(8,128)(2,1)S(1)}, bf16[256,256]{1,0:T(8,128)(2,1)S(1)}, u32[]{:S(2)}, u32[]{:S(2)}) collective-permute-start(bf16[256,256]{1,0:T(8,128)(2,1)S(1)} %get-tuple-element.362), channel_id=1, source_target_pairs={{0,4},{4,8},{8,12},{12,16},{16,20},{20,24},{24,28},{28,0},{1,5},{5... | collective-permute-start | bytes 393224 | tf_op jit(solution)/shard_map/while/body/eval_jaxpr/ppermute | solution.py:9
  64.4 7.7 %collective-permute-start = (bf16[256,256]{1,0:T(8,128)(2,1)S(1)}, bf16[256,256]{1,0:T(8,128)(2,1)S(1)}, u32[]{:S(2)}, u32[]{:S(2)}) collective-permute-start(bf16[256,256]{1,0:T(8,128)(2,1)S(1)} %get-tuple-element.362), channel_id=1, source_target_pairs={{0,4},{4,8},{8,12},{12,16},{16,20},{20,24},{24,28},{28,0},{1,5},{5... | collective-permute-start | bytes 393224 | tf_op jit(solution)/shard_map/while/body/eval_jaxpr/ppermute | solution.py:9
  73.8 7.7 %collective-permute-start = (bf16[256,256]{1,0:T(8,128)(2,1)S(1)}, bf16[256,256]{1,0:T(8,128)(2,1)S(1)}, u32[]{:S(2)}, u32[]{:S(2)}) collective-permute-start(bf16[256,256]{1,0:T(8,128)(2,1)S(1)} %get-tuple-element.362), channel_id=1, source_target_pairs={{0,4},{4,8},{8,12},{12,16},{16,20},{20,24},{24,28},{28,0},{1,5},{5... | collective-permute-start | bytes 393224 | tf_op jit(solution)/shard_map/while/body/eval_jaxpr/ppermute | solution.py:9
  84.0 55.0 %all-reduce.3.cloned.1.call-start = ((), (), s32[]{:S(2)}) async-start(), calls=%async_computation.2 | async-start | bytes 524288 | tf_op jit(solution)/shard_map/psum | solution.py:62
  105.8 107.1 %all-reduce.5.cloned.1.call-start = ((), (), s32[]{:S(2)}) async-start(), calls=%async_computation.3 | async-start | bytes 524288 | tf_op jit(solution)/shard_map/psum | solution.py:62
  139.0 0.9 copy-start.1
  139.0 1.0 copy-start.2
Sparse Core Ops, SparseCore 0:
  84.1 19.7 reduce-scatter.1
  107.0 31.9 all-reduce.2
  142.3 70.5 all-reduce.4
